TPU v7x, 512 devices: a whole 4x8x8 slice. The times are simulated.
512 devices in a mesh: island: 16 (over y, core), fsdp: 32 (over z, x).
Axes of the slice: x: 4, y: 8, z: 8, core: 2. Of those that a mesh axis runs over, the one named last changes fastest.
Arguments:
- delta: bfloat16 [16, 2048, 4096], P('island', 'fsdp'), may hold values from -6 to 6
- error: float32 [16, 2048, 4096], P('island', 'fsdp'), may hold values from -6 to 6
- param: bfloat16 [2048, 4096], P('fsdp'), may hold values from -6 to 6
- velocity: bfloat16 [2048, 4096], P('fsdp'), may hold values from -4 to 4
- piece_ids: int32 [32, 32, 16], P('fsdp'), may hold values from 0 to 2047, as said below
- piece_counts: int32 [32, 32], P('fsdp'), may hold values from 8 to 16, as said below
Outputs:
- new_error: float32 [16, 2048, 4096], P('island', 'fsdp')
- new_param: bfloat16 [2048, 4096], P('fsdp')
- new_velocity: bfloat16 [2048, 4096], P('fsdp')
- compressed: float32 [32, 32, 16, 128], P('fsdp')
Inputs may be any that keep to these rules, and one draw needn't show every extreme that they name: `piece_ids`: within one shard's lists all entries are distinct, entries past the count included; those are ignored. `piece_counts`: one owner receives exactly 16 live entries from every shard.
All inputs are finite; a program needn't handle non-finite values.
Results may differ from a plain program's by a relative error of at most 0.001.
Values sent between devices are 32-bit elements; how exact they have to be, the bound alone decides.
A program may use at most 64 MiB of HBM per device.

v0:
```python
import jax
import jax.numpy as jnp
from jax import lax
from jax.sharding import PartitionSpec as P

decay_rate = 0.9
outer_rate = 0.7
nesterov = 0.9
eps_value = 1e-06


def cosine_table(side):
    freq = jnp.arange(side, dtype=jnp.int32)[:, None].astype(jnp.float32)
    place = jnp.arange(side, dtype=jnp.int32)[None, :].astype(jnp.float32)
    scale = jnp.where(freq == 0.0, jnp.sqrt(1.0 / side), jnp.sqrt(2.0 / side))
    return scale * jnp.cos(jnp.pi * (2.0 * place + 1.0) * freq / (2.0 * side))


def transform(field, table, column_table):
    rows, width = field.shape
    side = table.shape[0]
    right = jnp.dot(field.reshape(-1, 128), column_table, precision=lax.Precision.HIGHEST)
    right = right.reshape(rows // side, side, width // 128, 128)
    left = jnp.einsum("kn,rnqj->rqkj", table, right, precision=lax.Precision.HIGHEST)
    return left.reshape(-1, 128)


def inverse(pieces, table, column_table, rows, width):
    side = table.shape[0]
    blocks = pieces.reshape(rows // side, width // 128, side, 128)
    left = jnp.einsum("kn,rqkj->rnqj", table, blocks, precision=lax.Precision.HIGHEST)
    back = jnp.dot(left.reshape(-1, 128), column_table.T, precision=lax.Precision.HIGHEST)
    return back.reshape(rows, width)


def normalize(values):
    return values / jnp.sqrt(jnp.mean(values * values, axis=-1, keepdims=True) + eps_value)


def island_norm(pieces):
    total = lax.psum(pieces, "island")
    return normalize(total)


def shards(delta, error, param, velocity, piece_ids, piece_counts):
    rows, width = param.shape
    table = cosine_table(64)
    column_table = jnp.kron(jnp.eye(2, dtype=jnp.float32), table.T)
    momentum = decay_rate * error[0] + delta[0].astype(jnp.float32)
    coefficients = transform(momentum, table, column_table)
    piece_list = piece_ids[0]
    owners, slots = piece_list.shape
    slot_index = jnp.arange(slots, dtype=jnp.int32)[None, :]
    active = (slot_index < piece_counts[0][:, None]).astype(jnp.float32)
    chosen = coefficients[piece_list] * active[..., None]
    flat_ids = piece_list.reshape(-1)
    arrived = lax.all_to_all(chosen, "fsdp", split_axis=0, concat_axis=0, tiled=True)
    compressed = island_norm(arrived)
    returned = lax.all_to_all(compressed, "fsdp", split_axis=0, concat_axis=0, tiled=True)
    kept_mask = (
        jnp.zeros((coefficients.shape[0],), jnp.float32).at[flat_ids].set(active.reshape(-1))
    )
    new_error = momentum - inverse(
        coefficients * kept_mask[:, None], table, column_table, rows, width
    )
    scattered = (
        jnp.zeros(coefficients.shape, jnp.float32).at[flat_ids].add(returned.reshape(-1, 128))
    )
    update = inverse(scattered, table, column_table, rows, width)
    moved = nesterov * velocity.astype(jnp.float32) + update
    new_velocity = moved.astype(jnp.bfloat16)
    new_param = (param.astype(jnp.float32) - outer_rate * (update + nesterov * moved)).astype(
        jnp.bfloat16
    )
    return (new_error[None], new_param, new_velocity, compressed[None])


def solution(mesh):
    in_specs = (
        P("island", "fsdp", None),
        P("island", "fsdp", None),
        P("fsdp", None),
        P("fsdp", None),
        P("fsdp", None, None),
        P("fsdp", None),
    )
    out_specs = (
        P("island", "fsdp", None),
        P("fsdp", None),
        P("fsdp", None),
        P("fsdp", None, None, None),
    )
    return jax.shard_map(shards, mesh=mesh, in_specs=in_specs, out_specs=out_specs, check_vma=False)
```

profile of v0, /device:TPU:24, one launch (start us, length us, event | category | flops | bytes accessed | tf_op | source)
XLA Modules:
  0.0 192.9 jit_solution(322883646928115541)
XLA Ops:
  7.2 0.8 compare_select_fusion
  8.1 0.7 fusion.26
  9.4 1.3 fusion.6
  10.9 1.6 fusion.2
  12.6 1.2 fusion.12
  13.8 1.0 gather_fusion
  14.8 0.8 broadcast_multiply_fusion
  15.7 13.2 %all-to-all-start = ((f32[32,16,128]{2,1,0:T(8,128)}), f32[32,16,128]{2,1,0:T(8,128)S(1)}, u32[]{:S(2)}, u32[]{:S(2)}) async-start(f32[32,16,128]{2,1,0:T(8,128)} %broadcast_multiply_fusion), calls=%async_computation | async-start | bytes 524288 | tf_op jit(solution)/shard_map/all_to_all | solution.py:57
  29.8 2.5 %scatter_custom_fusion = f32[2048]{0:T(1024)S(1)} fusion(s32[512]{0:T(512)S(1)} %bitcast.60, f32[512]{0:T(512)S(1)} %reshape.275, f32[]{:T(128)} %constant.13.clone.1), kind=kCustom, calls=%fused_computation.46 | custom fusion | bytes 8196 | tf_op jit(solution)/shard_map/scatter | solution.py:61
  32.4 1.3 convolution_bitcast_fusion.1
  34.3 7.2 %all-to-all-done = f32[32,16,128]{2,1,0:T(8,128)S(1)} async-done(((f32[32,16,128]{2,1,0:T(8,128)}), f32[32,16,128]{2,1,0:T(8,128)S(1)}, u32[]{:S(2)}, u32[]{:S(2)}) %all-to-all-start) | async-done | bytes 262176 | tf_op jit(solution)/shard_map/all_to_all | solution.py:57
  42.3 1.0 fusion.32
  43.5 107.5 %all-reduce.2.cloned.1.call-done = f32[32,16,128]{2,1,0:T(8,128)} async-done(((f32[32,16,128]{2,1,0:T(8,128)}), f32[32,16,128]{2,1,0:T(8,128)}) %all-reduce.2.cloned.1.call-update) | async-done | bytes 262160 | tf_op jit(solution)/shard_map/psum | solution.py:41
  151.0 1.1 multiply_reduce_fusion
  152.1 1.8 broadcast_divide_fusion
  153.9 10.2 %all-to-all-start.1 = ((f32[32,16,128]{2,1,0:T(8,128)}), f32[32,16,128]{2,1,0:T(8,128)S(1)}, u32[]{:S(2)}, u32[]{:S(2)}) async-start(f32[32,16,128]{2,1,0:T(8,128)} %broadcast_divide_fusion), calls=%async_computation.1 | async-start | bytes 524288 | tf_op jit(solution)/shard_map/all_to_all | solution.py:59
  164.1 1.1 fusion.5
  165.3 0.8 fusion.41
  166.1 11.9 %all-to-all-done.1 = f32[32,16,128]{2,1,0:T(8,128)S(1)} async-done(((f32[32,16,128]{2,1,0:T(8,128)}), f32[32,16,128]{2,1,0:T(8,128)S(1)}, u32[]{:S(2)}, u32[]{:S(2)}) %all-to-all-start.1) | async-done | bytes 262176 | tf_op jit(solution)/shard_map/all_to_all | solution.py:59
  178.0 2.7 %scatter_custom_fusion.1 = f32[2048,128]{1,0:T(8,128)S(1)} fusion(s32[512]{0:T(512)S(1)} %bitcast.61, f32[512,128]{1,0:T(8,128)S(1)} %bitcast.59, f32[]{:T(128)} %constant.13.clone.1), kind=kCustom, calls=%fused_computation.15 | custom fusion | flops 65536 | bytes 1048580 | tf_op jit(solution)/shard_map/scatter-add | solution.py:67
  180.6 1.3 convolution_bitcast_fusion
  182.5 1.0 fusion.33
  183.8 0.8 copy-done.4
  184.7 1.3 fusion.4
  (37 shorter events, 4.4 us)
Async XLA Ops:
  7.2 2.2 %copy-start.2 = (bf16[1,64,4096]{2,1,0:T(8,128)(2,1)S(1)}, bf16[1,64,4096]{2,1,0:T(8,128)(2,1)}, u32[]{:S(2)}) copy-start(bf16[1,64,4096]{2,1,0:T(8,128)(2,1)} %param.6) | copy-start | bytes 1572868
  15.7 25.9 %all-to-all-start = ((f32[32,16,128]{2,1,0:T(8,128)}), f32[32,16,128]{2,1,0:T(8,128)S(1)}, u32[]{:S(2)}, u32[]{:S(2)}) async-start(f32[32,16,128]{2,1,0:T(8,128)} %broadcast_multiply_fusion), calls=%async_computation | async-start | bytes 524288 | tf_op jit(solution)/shard_map/all_to_all | solution.py:57
  28.9 0.7 copy-start.6
  28.9 122.1 %all-reduce.2.cloned.1.call-start = ((), (), s32[]{:S(2)}) async-start(), calls=%async_computation.2 | async-start | bytes 524288 | tf_op jit(solution)/shard_map/psum | solution.py:41
  41.5 0.7 copy-start.3
  43.5 120.7 %copy-start = (f32[1,64,4096]{2,1,0:T(8,128)S(1)}, f32[1,64,4096]{2,1,0:T(8,128)}, u32[]{:S(2)}) copy-start(f32[1,64,4096]{2,1,0:T(8,128)} %param.7) | copy-start | bytes 3145732
  153.9 24.0 %all-to-all-start.1 = ((f32[32,16,128]{2,1,0:T(8,128)}), f32[32,16,128]{2,1,0:T(8,128)S(1)}, u32[]{:S(2)}, u32[]{:S(2)}) async-start(f32[32,16,128]{2,1,0:T(8,128)} %broadcast_divide_fusion), calls=%async_computation.1 | async-start | bytes 524288 | tf_op jit(solution)/shard_map/all_to_all | solution.py:59
  164.1 1.1 copy-start.1
  183.5 1.0 copy-start.4
  183.6 1.2 copy-start.5
Sparse Core Ops, SparseCore 0:
  42.4 108.5 all-reduce.1
where the time goes:
time: 193 us
  waiting for transfers between devices  127 us (66%)
  starting transfers between devices  23.4 us (12%)
  between operations  14.3 us (7%)
  other arithmetic  12.8 us (7%)
  local copies, waits for them, and re-layouts  8.35 us (4%)
  matrix products  7.44 us (4%)
    psum x1, waiting for transfers between devices, island_norm(): total = lax.psum(pieces, 'island')  108 us
    all_to_all x1, starting transfers between devices, shards(): lax.all_to_all(chosen, 'fsdp', split_axis=0, concat_axis=0, tiled=True)  13.2 us
    all_to_all x1, waiting for transfers between devices, shards(): lax.all_to_all(compressed, 'fsdp', split_axis=0, concat_axis=0, tiled=True)  11.9 us
    all_to_all x1, starting transfers between devices, shards(): lax.all_to_all(compressed, 'fsdp', split_axis=0, concat_axis=0, tiled=True)  10.2 us
    all_to_all x1, waiting for transfers between devices, shards(): lax.all_to_all(chosen, 'fsdp', split_axis=0, concat_axis=0, tiled=True)  7.21 us
  transfers between devices with their start and end apart: 3, of which 3 were waited for; matrix products, arithmetic and copies ran while one was open for 4% of the time, Pallas kernels for 0%

commit v1 on v0

--- a/solution.py
+++ b/solution.py
@@ -38,7 +38,7 @@
 
 
 def island_norm(pieces):
-    total = lax.psum(pieces, "island")
+    total = jnp.sum(lax.all_gather(pieces, "island"), axis=0)
     return normalize(total)
 
 

time: 193 us -> 121 us (0.63)
  the two profiles are of different devices: /device:TPU:24 before, /device:TPU:8 now
where the time goes in v1:
time: 121 us; the launch traced here: 120 us
  waiting for transfers between devices  45.2 us (37%)
  blocking collectives  25.8 us (21%)
  between operations  14.3 us (12%)
  other arithmetic  11.3 us (9%)
  starting transfers between devices  10.4 us (9%)
  matrix products  7.45 us (6%)
  local copies, waits for them, and re-layouts  6.11 us (5%)
    all_gather x1, waiting for transfers between devices, island_norm(): total = jnp.sum(lax.all_gather(pieces, 'island'), axis=0)  34 us
    all_to_all x1, blocking collectives, shards(): lax.all_to_all(chosen, 'fsdp', split_axis=0, concat_axis=0, tiled=True)  25.8 us
    all_to_all x1, waiting for transfers between devices, shards(): lax.all_to_all(compressed, 'fsdp', split_axis=0, concat_axis=0, tiled=True)  11.2 us
    all_to_all x1, starting transfers between devices, shards(): lax.all_to_all(compressed, 'fsdp', split_axis=0, concat_axis=0, tiled=True)  10.4 us
    dot_general x2, matrix products, inverse(): jnp.einsum('kn,rqkj->rnqj', table, blocks, precision=lax.Precision.HIGHEST)  2.61 us
    scatter-add x1, other arithmetic, shards(): jnp.zeros(coefficients.shape, jnp.float32).at[flat_ids]  2.5 us
    reduce_sum x1, other arithmetic, island_norm(): total = jnp.sum(lax.all_gather(pieces, 'island'), axis=0)  2.48 us
    scatter x1, local copies, waits for them, and re-layouts, shards(): jnp.zeros((coefficients.shape[0],), jnp.float32).at[flat_ids]  2.45 us
  transfers between devices with their start and end apart: 2, of which 2 were waited for; matrix products, arithmetic and copies ran while one was open for 7% of the time, Pallas kernels for 0%

profile of v1, /device:TPU:8, one launch (start us, length us, event | category | flops | bytes accessed | tf_op | source)
XLA Modules:
  0.0 120.5 jit_solution(17562646884701062201)
XLA Ops:
  7.2 0.2 cosine_multiply_fusion.4
  7.8 1.5 %fusion.6 = f32[8,8,32,128]{3,1,2,0:T(8,128)S(1)} fusion(bf16[1,64,4096]{2,1,0:T(8,128)(2,1)} %param.6, f32[1,64,4096]{2,1,0:T(8,128)} %param.7), kind=kLoop, calls=%fused_computation.14 | loop fusion | flops 786432 | bytes 2621440
  9.5 1.7 %fusion.2 = f32[64,32,128]{2,0,1:T(8,128)S(1)} fusion(f32[128,128,1]{1,0,2:T(8,128)S(1)} %reshape.296, f32[64,32,128]{2,1,0:T(8,128)S(1)} %bitcast.56), kind=kOutput, calls=%fused_computation.7 | convolution fusion | flops 402653184 | bytes 2162688 | tf_op jit(solution)/shard_map/dot_general | solution.py:22
  11.1 1.2 %fusion.12 = f32[32,128,64]{1,2,0:T(8,128)S(1)} fusion(f32[64,32,128]{2,0,1:T(8,128)S(1)} %fusion.2, f32[64]{0:T(128)S(1)} %iota_convert_fusion, f32[64]{0:T(128)S(1)} %get-tuple-element.7, f32[64]{0:T(128)S(1)} %get-tuple-element.6), kind=kOutput, calls=%fused_computation.25 | convolution fusion | flops 201338880 | bytes 2097920 | tf_op jit(solution)/shard_map/kn,rnqj->rqkj/dot_general | solution.py:24
  12.6 1.0 gather_fusion
  13.8 25.8 %all_to_all.10 = f32[32,16,128]{2,1,0:T(8,128)} all-to-all(f32[32,16,128]{2,1,0:T(8,128)S(1)} %broadcast_multiply_fusion), channel_id=1, replica_groups=mesh['island'=16,'fsdp'=32] {'fsdp'}, dimensions={0} | all-to-all | bytes 524288 | tf_op jit(solution)/shard_map/all_to_all | solution.py:57
  40.0 2.5 %scatter_custom_fusion = f32[2048]{0:T(1024)S(1)} fusion(s32[512]{0:T(512)S(1)} %bitcast.61, f32[512]{0:T(512)S(1)} %reshape.282, f32[]{:T(128)} %constant.13.clone.1), kind=kCustom, calls=%fused_computation.47 | custom fusion | bytes 8196 | tf_op jit(solution)/shard_map/scatter | solution.py:61
  42.5 1.3 %convolution_bitcast_fusion.1 = f32[1,64,32,128]{3,1,2,0:T(8,128)S(1)} fusion(f32[32,128,64]{1,2,0:T(8,128)S(1)} %fusion.12, f32[32,64]{1,0:T(8,128)S(1)} %mul.237, f32[64]{0:T(128)S(1)} %iota_convert_fusion, f32[64]{0:T(128)S(1)} %get-tuple-element.7, f32[64]{0:T(128)S(1)} %get-tuple-element.6), kind=kOutput, calls=%fused_computation.4 | convolution fusion | flops 201601024 | bytes 2106112 | tf_op jit(solution)/shard_map/kn,rqkj->rnqj/dot_general | solution.py:31
  43.8 0.6 copy.22
  44.5 1.0 fusion.32
  45.5 0.2 reshape.263
  45.7 34.0 %all-gather.3.cloned.1.call-done = f32[512,16,128]{2,1,0:T(8,128)} async-done(((f32[32,16,128]{2,1,0:T(8,128)}), f32[512,16,128]{2,1,0:T(8,128)}) %all-gather.3.cloned.1.call-update) | async-done | bytes 4194320 | tf_op jit(solution)/shard_map/all_gather | solution.py:41
  79.6 2.5 %reduce_sum.20 = f32[32,16,128]{2,1,0:T(8,128)S(1)} reduce(f32[16,32,16,128]{3,2,1,0:T(8,128)} %bitcast.54, f32[]{:T(128)} %constant.13.clone.1), dimensions={0}, to_apply=%region_1.2 | reduce | flops 983040 | bytes 4456452 | tf_op jit(solution)/shard_map/reduce_sum | solution.py:41
  82.3 0.8 broadcast_divide_fusion
  83.1 10.4 %all-to-all-start.1 = ((f32[32,16,128]{2,1,0:T(8,128)}), f32[32,16,128]{2,1,0:T(8,128)S(1)}, u32[]{:S(2)}, u32[]{:S(2)}) async-start(f32[32,16,128]{2,1,0:T(8,128)} %broadcast_divide_fusion), calls=%async_computation.1 | async-start | bytes 524288 | tf_op jit(solution)/shard_map/all_to_all | solution.py:59
  93.5 1.1 fusion.5
  94.6 0.8 bitcast_divide_fusion
  95.5 11.2 %all-to-all-done.1 = f32[32,16,128]{2,1,0:T(8,128)S(1)} async-done(((f32[32,16,128]{2,1,0:T(8,128)}), f32[32,16,128]{2,1,0:T(8,128)S(1)}, u32[]{:S(2)}, u32[]{:S(2)}) %all-to-all-start.1) | async-done | bytes 262176 | tf_op jit(solution)/shard_map/all_to_all | solution.py:59
  106.7 2.5 %scatter_custom_fusion.1 = f32[2048,128]{1,0:T(8,128)S(1)} fusion(s32[512]{0:T(512)S(1)} %bitcast.62, f32[512,128]{1,0:T(8,128)S(1)} %bitcast.60, f32[]{:T(128)} %constant.13.clone.1), kind=kCustom, calls=%fused_computation.15 | custom fusion | flops 65536 | bytes 1048580 | tf_op jit(solution)/shard_map/scatter-add | solution.py:67
  109.2 1.3 %convolution_bitcast_fusion = f32[1,64,32,128]{3,1,2,0:T(8,128)S(1)} fusion(f32[32,64,128]{2,1,0:T(8,128)S(1)} %bitcast.55, f32[64]{0:T(128)S(1)} %iota_convert_fusion, f32[64]{0:T(128)S(1)} %get-tuple-element.7, f32[64]{0:T(128)S(1)} %get-tuple-element.6), kind=kOutput, calls=%fused_computation.3 | convolution fusion | flops 201338880 | bytes 2097920 | tf_op jit(solution)/shard_map/kn,rqkj->rnqj/dot_general | solution.py:31
  110.5 0.6 copy.24
  111.1 1.0 fusion.33
  112.1 0.2 reshape.268
  112.3 1.3 %fusion.4 = (bf16[64,4096]{1,0:T(8,128)(2,1)}, bf16[64,4096]{1,0:T(8,128)(2,1)}) fusion(f32[64,4096]{1,0:T(8,128)S(1)} %reshape.268, bf16[64,4096]{1,0:T(8,128)(2,1)S(1)} %copy-done.2, bf16[64,4096]{1,0:T(8,128)(2,1)S(1)} %copy-done.3), kind=kLoop, calls=%fused_computation.11 | loop fusion | flops 2621440 | bytes 3145728 | tf_op jit(solution)/shard_map/convert_element_type | solution.py:71
  (35 shorter events, 1.6 us)
Async XLA Ops:
  7.2 72.5 %all-gather.3.cloned.1.call-start = ((), (), s32[]{:S(2)}) async-start(), calls=%async_computation.2 | async-start | bytes 4456448 | tf_op jit(solution)/shard_map/all_gather | solution.py:41
  7.8 4.6 %copy-start.5 = (s32[1,32]{1,0:T(1,128)S(1)}, s32[1,32]{1,0:T(1,128)}, u32[]{:S(2)}) copy-start(s32[1,32]{1,0:T(1,128)} %param.11) | copy-start | bytes 388
  7.8 4.7 %copy-start.4 = (s32[1,32,16]{1,2,0:T(8,128)S(1)}, s32[1,32,16]{1,2,0:T(8,128)}, u32[]{:S(2)}) copy-start(s32[1,32,16]{1,2,0:T(8,128)} %param.10) | copy-start | bytes 6148
  45.4 48.1 %copy-start = (f32[1,64,4096]{2,1,0:T(8,128)S(1)}, f32[1,64,4096]{2,1,0:T(8,128)}, u32[]{:S(2)}) copy-start(f32[1,64,4096]{2,1,0:T(8,128)} %param.7) | copy-start | bytes 3145732
  45.7 47.9 %copy-start.1 = (bf16[1,64,4096]{2,1,0:T(8,128)(2,1)S(1)}, bf16[1,64,4096]{2,1,0:T(8,128)(2,1)}, u32[]{:S(2)}) copy-start(bf16[1,64,4096]{2,1,0:T(8,128)(2,1)} %param.6) | copy-start | bytes 1572868
  83.1 23.6 %all-to-all-start.1 = ((f32[32,16,128]{2,1,0:T(8,128)}), f32[32,16,128]{2,1,0:T(8,128)S(1)}, u32[]{:S(2)}, u32[]{:S(2)}) async-start(f32[32,16,128]{2,1,0:T(8,128)} %broadcast_divide_fusion), calls=%async_computation.1 | async-start | bytes 524288 | tf_op jit(solution)/shard_map/all_to_all | solution.py:59
  109.2 3.1 %copy-start.2 = (bf16[64,4096]{1,0:T(8,128)(2,1)S(1)}, bf16[64,4096]{1,0:T(8,128)(2,1)}, u32[]{:S(2)}) copy-start(bf16[64,4096]{1,0:T(8,128)(2,1)} %param.9) | copy-start | bytes 1572868
  109.2 3.1 %copy-start.3 = (bf16[64,4096]{1,0:T(8,128)(2,1)S(1)}, bf16[64,4096]{1,0:T(8,128)(2,1)}, u32[]{:S(2)}) copy-start(bf16[64,4096]{1,0:T(8,128)(2,1)} %param.8) | copy-start | bytes 1572868
Sparse Core Ops, SparseCore 0:
  39.7 39.8 all-gather.2
